TPU v7x, 512 devices: a whole 4x4x16 slice. The times are simulated.
512 devices in a mesh: frame: 4 (over y), vox: 128 (over x, z, core).
Axes of the slice: x: 4, y: 4, z: 16, core: 2. Of those that a mesh axis runs over, the one named last changes fastest.
Arguments:
- pool: bfloat16 [2048, 131072], P('frame', 'vox'), may hold values from -6 to 6
- dictionary: bfloat16 [1024, 131072], P(None, 'vox'), may hold values from -0.03314563 to 0.03314563
- support: int32 [1024, 1024], P(None, 'vox'), may hold values from 0 to 1, as said below
- pick: int32 [1024], P('frame'), may hold values from 0 to 511
Outputs:
- codes: bfloat16 [1024, 1024], P('frame')
- gradient: float32 [1024, 131072], P('frame', 'vox')
Inputs may be any that keep to these rules, and one draw needn't show every extreme that they name: Every mode has at least one voxel block in its support.
All inputs are finite; a program needn't handle non-finite values.
Results may differ from a plain program's by a relative error of at most 0.015.
Values may be sent and summed in bfloat16 or wider, within the bound.
A program may use at most 64 MiB of HBM per device.

v0:
```python
import jax
import jax.numpy as jnp
from jax import lax
from jax.sharding import PartitionSpec as P

BLOCK = 128


def shrink(value, limit):
    return jnp.sign(value) * jnp.maximum(jnp.abs(value) - limit, 0.0)


def against(left, right):
    return lax.dot_general(
        left, right, (((1,), (1,)), ((), ())), preferred_element_type=jnp.float32
    )


def body(pool, dictionary, support, pick):
    batch = pool[pick]
    batch_wide = batch.astype(jnp.float32)
    keep = jnp.repeat(support, BLOCK, axis=1).astype(jnp.bfloat16)
    masked = dictionary * keep
    corr_local = against(batch, masked)
    energy_local = jnp.sum(jnp.square(masked.astype(jnp.float32)), axis=1)
    corr, energy = lax.psum((corr_local, energy_local), "vox")
    step = 1.0 / (energy + 1e-05)
    first = shrink(corr * step, 0.3 * step).astype(jnp.bfloat16)
    resid = (jnp.dot(first, masked, preferred_element_type=jnp.float32) - batch_wide).astype(
        jnp.bfloat16
    )
    push = lax.psum(against(resid, masked), "vox")
    codes = shrink(first.astype(jnp.float32) - step * push, 0.3 * step).astype(jnp.bfloat16)
    error = (jnp.dot(codes, masked, preferred_element_type=jnp.float32) - batch_wide).astype(
        jnp.bfloat16
    )
    groups = lax.axis_size("frame")
    own_rows = support.shape[0] // groups
    summed = lax.psum_scatter(
        lax.dot_general(
            codes, error, (((0,), (0,)), ((), ())), preferred_element_type=jnp.float32
        ).astype(jnp.bfloat16),
        "frame",
        scatter_dimension=0,
        tiled=True,
    ).astype(jnp.float32)
    keep_rows = lax.dynamic_slice_in_dim(keep, lax.axis_index("frame") * own_rows, own_rows, 0)
    gradient = keep_rows.astype(jnp.float32) * summed / (batch.shape[0] * groups)
    return (codes, gradient)


def solution(mesh):
    placed = (P("frame", "vox"), P(None, "vox"), P(None, "vox"), P("frame"))
    return jax.shard_map(
        body,
        mesh=mesh,
        in_specs=placed,
        out_specs=(P("frame", None), P("frame", "vox")),
        check_vma=False,
    )
```

profile of v0, /device:TPU:1, one launch (start us, length us, event | category | flops | bytes accessed | tf_op | source)
XLA Modules:
  0.0 748.9 jit_solution(16219456594878112621)
XLA Ops:
  7.2 0.0 copy-start
  7.2 0.0 all-reduce.3.cloned.1.call-start
  7.2 0.8 convert_element_type.37
  8.1 0.2 copy.6
  8.2 0.0 copy-start.1
  8.3 0.8 compare_select_fusion
  9.1 2.9 broadcast_in_dim.5
  12.0 0.0 copy-done.1
  12.0 2.1 multiply_reduce_fusion
  14.1 0.0 copy-done
  14.1 2.0 gather_fusion
  16.1 3.5 fusion.5
  19.6 0.0 all-reduce.3.cloned.1.call-update
  19.6 0.0 all-reduce.5.cloned.1.call-start
  19.6 254.5 %psum.22 = f32[1024]{0:T(1024)S(1)} all-reduce(f32[1024]{0:T(1024)S(1)} %get-tuple-element.2), channel_id=1, replica_groups=mesh['frame'=4,'vox'=128] {'vox'}, use_global_device_ids=true, to_apply=%region_2.0 | all-reduce | flops 1024 | bytes 8192 | tf_op jit(solution)/shard_map/psum | solution.py:26
  274.1 85.5 %all-reduce.3.cloned.1.call-done = f32[256,1024]{1,0:T(8,128)} async-done(((f32[256,1024]{1,0:T(8,128)}), f32[256,1024]{1,0:T(8,128)}) %all-reduce.3.cloned.1.call-update) | async-done | bytes 1048592 | tf_op jit(solution)/shard_map/psum | solution.py:26
  359.7 5.1 fusion.2
  364.8 0.0 all-reduce.5.cloned.1.call-update
  364.8 0.0 reduce-scatter.2.cloned.1.call-start
  364.9 332.1 %all-reduce.5.cloned.1.call-done = f32[256,1024]{1,0:T(8,128)} async-done(((f32[256,1024]{1,0:T(8,128)}), f32[256,1024]{1,0:T(8,128)}) %all-reduce.5.cloned.1.call-update) | async-done | bytes 1048592 | tf_op jit(solution)/shard_map/psum | solution.py:32
  697.0 3.2 multiply_convert_fusion
  700.2 4.5 convolution_convert_fusion
  704.7 0.0 reduce-scatter.2.cloned.1.call-update
  704.8 2.0 copy.12
  706.8 33.2 %reduce-scatter.2.cloned.1.call-done = bf16[256,1024]{1,0:T(8,128)(2,1)} async-done(((bf16[1024,1024]{1,0:T(8,128)(2,1)}), bf16[256,1024]{1,0:T(8,128)(2,1)}) %reduce-scatter.2.cloned.1.call-update) | async-done | bytes 524304 | tf_op jit(solution)/shard_map/reduce_scatter | solution.py:39
  740.0 2.4 multiply_multiply_fusion
  (2 shorter events, 0.0 us)
Async XLA Ops:
  7.2 7.0 copy-start
  7.2 352.5 %all-reduce.3.cloned.1.call-start = ((), (), s32[]{:S(2)}) async-start(), calls=%async_computation.1 | async-start | bytes 2097152 | tf_op jit(solution)/shard_map/psum | solution.py:26
  8.2 3.8 copy-start.1
  19.6 677.4 %all-reduce.5.cloned.1.call-start = ((), (), s32[]{:S(2)}) async-start(), calls=%async_computation.2 | async-start | bytes 2097152 | tf_op jit(solution)/shard_map/psum | solution.py:32
  364.8 375.2 %reduce-scatter.2.cloned.1.call-start = ((), (), s32[]{:S(2)}) async-start(), calls=%async_computation.3 | async-start | bytes 2621440 | tf_op jit(solution)/shard_map/reduce_scatter | solution.py:39
Sparse Core Ops, SparseCore 0:
  19.7 339.9 all-reduce.2
  364.9 332.0 all-reduce.4
  704.9 35.0 reduce-scatter.1
where the time goes:
time: 749 us
  waiting for transfers between devices  451 us (60%)
  blocking collectives  254 us (34%)
  between operations  13.8 us (2%)
  matrix products  13.1 us (2%)
  other arithmetic  9.34 us (1%)
    psum x1, waiting for transfers between devices, body(): push = lax.psum(against(resid, masked), 'vox')  332 us
    psum x1, blocking collectives, body(): corr, energy = lax.psum((corr_local, energy_local), 'vox')  254 us
    psum x1, waiting for transfers between devices, body(): corr, energy = lax.psum((corr_local, energy_local), 'vox')  85.5 us
    reduce_scatter x1, waiting for transfers between devices, body(): lax.psum_scatter(lax.dot_general(codes, error, (((0,), (0,)), ((), ())),...  33.2 us
  transfers between devices with their start and end apart: 3, of which 3 were waited for; matrix products, arithmetic and copies ran while one was open for 0% of the time, Pallas kernels for 0%

commit v1 on v0

v1 whole, which is shorter than its diff:
```python
import jax
import jax.numpy as jnp
from jax import lax
from jax.experimental import pallas as pl
from jax.experimental.pallas import tpu as pltpu
from jax.sharding import PartitionSpec as P

MESH = pl.DeviceIdType.MESH
NX, NY, NZ = 4, 4, 16
FAR = (8, 7, 9, 6, 10, 5, 11, 4, 12, 3, 13, 2, 14, 1, 15, 0)
OFFS = (2, 1, 3)
PLANE = tuple((i, j) for i in (2, 1, 3, 0) for j in (2, 1, 3, 0) if i or j)
BF, F32 = jnp.bfloat16, jnp.float32


def shrink(value, limit):
    return jnp.where(value < 0, -1.0, 1.0) * jnp.maximum(jnp.abs(value) - limit, 0.0)


def mm_t(left, right):
    return lax.dot_general(left, right, (((1,), (1,)), ((), ())), preferred_element_type=F32)


def mm_0(left, right):
    return lax.dot_general(left, right, (((0,), (0,)), ((), ())), preferred_element_type=F32)


def column(row):
    return jnp.transpose(jnp.broadcast_to(row, (128, 128)))


def kernel(
    pool, dico, supt, pick, codes_out, grad_out,
    masked, batch, psend, pown, precv, xsend, xrecv, zsend, zrecv, zown, zall,
    e_own, e_core, e_x, e_xr, e_z, e_zr, e_step, fall, gmat, call, error,
    s_b, r_b, s_p, r_p, s_ec, r_ec, s_ex, r_ex, s_ez, r_ez, s_x, r_x, s_z, r_z, s_a, r_a,
    s_f, r_f, s_fc, r_fc, s_g, r_g, s_c, r_c, s_cc, r_cc,
):
    y, v = lax.axis_index("frame"), lax.axis_index("vox")
    x, z, c = v // 32, (v // 2) % NZ, v % 2

    def dev(xx, yy, zz, cc):
        return (yy, (xx * NZ + zz) * 2 + cc)

    partner = dev(x, y, z, 1 - c)
    xs = [(x + i) % NX for i in OFFS]
    ys = [(y + i) % NY for i in OFFS]
    zs = [(z + o) % NZ for o in FAR]
    xpeer = [dev(xx, y, z, c) for xx in xs]
    ypeer = [dev(x, yy, z, c) for yy in ys]
    zpeer = [dev(x, y, zz, c) for zz in zs[:15]]
    plane = [((x + i) % NX, (y + j) % NY) for i, j in PLANE]
    ppeer = [dev(xx, yy, z, c) for xx, yy in plane]
    sent = []

    def send(src, dst, ssem, rsem, to):
        copy = pltpu.make_async_remote_copy(
            src_ref=src, dst_ref=dst, send_sem=ssem, recv_sem=rsem, device_id=to, device_id_type=MESH
        )
        copy.start()
        sent.append(copy)
        return copy

    barrier = pltpu.get_barrier_semaphore()
    everyone = [partner] + zpeer + ppeer
    for to in everyone:
        pl.semaphore_signal(barrier, inc=1, device_id=to, device_id_type=MESH)

    lane = lax.broadcasted_iota(jnp.int32, (128, 128), 1)
    mine = pl.multiple_of(y * 256, 256)
    for r in range(2):
        rows = column(pick[:, 128 * r : 128 * (r + 1)])
        hot = jnp.concatenate([(rows == lane + 128 * j).astype(F32).astype(BF) for j in range(4)], axis=1)
        batch[pl.ds(pl.multiple_of(y * 256 + 128 * r, 128), 128), :] = jnp.dot(
            hot, pool[...], preferred_element_type=F32
        ).astype(BF)

    block_of = lax.broadcasted_iota(jnp.int32, (8, 1024), 1) // 128
    spread = (block_of == lax.broadcasted_iota(jnp.int32, (8, 1024), 0)).astype(F32).astype(BF)

    def keep_rows(start, count):
        return mm_0(supt[:, pl.ds(start, count)].astype(F32).astype(BF), spread)

    @pl.loop(0, 8)
    def _(j):
        rows = pl.multiple_of(j * 128, 128)
        kept = dico[pl.ds(rows, 128), :] * keep_rows(rows, 128).astype(BF)
        masked[pl.ds(rows, 128), :] = kept
        wide = kept.astype(F32)
        part = jnp.zeros((128, 128), F32)
        for b in range(8):
            piece = wide[:, 128 * b : 128 * (b + 1)]
            part += piece * piece
        e_own[pl.ds(j, 1), :] = jnp.sum(jnp.transpose(part), axis=0, keepdims=True)

    pl.semaphore_wait(barrier, len(everyone))
    own_batch = batch.at[pl.ds(mine, 256), :]
    b_copies = [send(own_batch, own_batch, s_b.at[k], r_b.at[k], ypeer[k]) for k in range(3)]
    ec = send(e_own, e_core, s_ec, r_ec, partner)

    def products(half, out, kind):
        rows = pl.ds(pl.multiple_of(half * 512, 512), 512)
        right = (batch[pl.ds(mine, 256), :], masked[pl.ds(mine, 256), :])
        for g in range(2):
            value = mm_t(masked[rows, :], right[g]).astype(kind)
            for xx in range(4):
                for zz in range(16):
                    top = xx * 128 + 16 * (zz // 2)
                    left = 128 * (zz % 2)
                    out[xx * 16 + zz, 16 * g : 16 * (g + 1), :] = value[top : top + 16, left : left + 128]

    products(1 - c, psend, BF)
    pc = send(psend, precv, s_p, r_p, partner)
    ec.wait_recv()
    e_x[...] = e_own[...] + e_core[...]
    ex = [send(e_x, e_xr.at[k], s_ex.at[k], r_ex.at[k], xpeer[k]) for k in range(3)]
    products(c, pown, F32)

    pc.wait_recv()
    xc = []
    for j in range(4):
        for k in range(3):
            for q in range(4):
                t = xs[k] * 16 + zs[4 * j + q]
                xsend[k, 4 * j + q] = (pown[t] + precv[t].astype(F32)).astype(BF)
            piece = pl.ds(4 * j, 4)
            xc.append(send(xsend.at[k, piece], xrecv.at[k, piece], s_x.at[k, j], r_x.at[k, j], xpeer[k]))
    for k in range(3):
        ex[k].wait_recv()
    e_z[...] = e_x[...] + e_xr[0] + e_xr[1] + e_xr[2]
    ez = [send(e_z, e_zr.at[n], s_ez.at[n], r_ez.at[n], zpeer[n]) for n in range(15)]

    zc = []
    for j in range(4):
        for k in range(3):
            xc[3 * j + k].wait_recv()
        for q in range(4):
            n = 4 * j + q
            t = x * 16 + zs[n]
            total = pown[t] + precv[t].astype(F32)
            for k in range(3):
                total += xrecv[k, n].astype(F32)
            if n < 15:
                zsend[n] = total.astype(BF)
                zc.append(send(zsend.at[n], zrecv.at[n], s_z.at[n], r_z.at[n], zpeer[n]))
            else:
                zown[...] = total
    for n in range(15):
        ez[n].wait_recv()
    energy = e_z[...]
    for n in range(15):
        energy += e_zr[n]
    e_step[...] = 1.0 / (energy + 1e-05)
    total = zown[...]
    for n in reversed(range(15)):
        zc[n].wait_recv()
        total += zrecv[n].astype(F32)
    zall[z] = total.astype(BF)
    za = [send(zall.at[z], zall.at[z], s_a.at[n], r_a.at[n], zpeer[n]) for n in range(15)]

    block = c * 4 + x
    step = column(e_step[pl.ds(block, 1), :])
    step = jnp.concatenate([step, step], axis=1)
    limit = 0.3 * step
    for n in range(15):
        za[n].wait_recv()

    def own_part(g):
        sides = [jnp.concatenate([zall[2 * r + h, 16 * g : 16 * (g + 1), :] for r in range(8)], axis=0) for h in range(2)]
        return jnp.concatenate(sides, axis=1)

    gmat[y] = own_part(1)
    gc = [send(gmat.at[y], gmat.at[y], s_g.at[k], r_g.at[k], ypeer[k]) for k in range(3)]
    corr = own_part(0).astype(F32)
    first = shrink(corr * step, limit).astype(BF)
    fall[block] = first
    fx = [send(fall.at[block], fall.at[block], s_f.at[k], r_f.at[k], xpeer[k]) for k in range(3)]
    fc = [send(fall.at[block], fall.at[block], s_fc.at[3], r_fc.at[3], partner)]
    for k in range(3):
        fx[k].wait_recv()
        came = c * 4 + (x + NX - OFFS[k]) % NX
        fc.append(send(fall.at[came], fall.at[came], s_fc.at[k], r_fc.at[k], partner))
    for copy in gc + fc:
        copy.wait_recv()
    push = -corr
    for g in range(4):
        push += jnp.dot(gmat[g], jnp.concatenate([fall[2 * g], fall[2 * g + 1]], axis=0), preferred_element_type=F32)
    codes = shrink(first.astype(F32) - step * push, limit)
    call[block, pl.ds(mine, 256), :] = jnp.transpose(codes).astype(BF)

    def slot(b, yy):
        return call.at[b, pl.ds(pl.multiple_of(yy * 256, 256), 256), :]

    own_slot = slot(block, y)
    cx = [send(own_slot, own_slot, s_c.at[k], r_c.at[k], ppeer[k]) for k in range(15)]
    cc = [send(own_slot, own_slot, s_cc.at[15], r_cc.at[15], partner)]

    order = (0, 1, 3, 2)
    for turn, j in enumerate(order):
        yy = (y + NY - j) % NY
        here = [k for k in range(15) if PLANE[k][1] == j]
        waits = list(cc) if j == 0 else []
        for k in here:
            cx[k].wait_recv()
            came = slot(c * 4 + (x + NX - PLANE[k][0]) % NX, yy)
            waits.append(send(came, came, s_cc.at[k], r_cc.at[k], partner))
        for copy in waits:
            copy.wait_recv()
        if j:
            b_copies[OFFS.index(j)].wait_recv()
        rows = pl.ds(pl.multiple_of(yy * 256, 256), 256)
        group = jnp.concatenate([call[b, rows, :] for b in range(8)], axis=1)
        if j == 0:
            codes_out[...] = group
        own_modes = jnp.concatenate([call[2 * y, rows, :], call[2 * y + 1, rows, :]], axis=1)
        for n in range(4):
            cols = slice(256 * n, 256 * (n + 1))
            rest = jnp.dot(group, masked[:, cols], preferred_element_type=F32) - batch[rows, cols].astype(F32)
            part = mm_0(own_modes, rest.astype(BF))
            if turn == 0:
                grad_out[:, cols] = part
            elif turn < 3:
                grad_out[:, cols] += part
            else:
                error[:, cols] = grad_out[:, cols] + part
    grad_out[...] = error[...] * keep_rows(mine, 256) * (1.0 / 1024)
    for copy in sent:
        copy.wait_send()


def body(pool, dictionary, support, pick):
    dma = pltpu.SemaphoreType.DMA
    sems = []
    for shape in ((3,), (), (), (3,), (15,), (3, 4), (15,), (15,), (3,), (4,), (3,), (15,), (16,)):
        sems += [dma(shape), dma(shape)]
    vmem = pl.BlockSpec(memory_space=pltpu.VMEM)
    return pl.pallas_call(
        kernel,
        out_shape=(jax.ShapeDtypeStruct((256, 1024), BF), jax.ShapeDtypeStruct((256, 1024), F32)),
        in_specs=[vmem] * 4,
        out_specs=(vmem, vmem),
        scratch_shapes=[
            pltpu.VMEM((1024, 1024), BF),
            pltpu.VMEM((1024, 1024), BF),
            pltpu.VMEM((64, 32, 128), BF),
            pltpu.VMEM((64, 32, 128), F32),
            pltpu.VMEM((64, 32, 128), BF),
            pltpu.VMEM((3, 16, 32, 128), BF),
            pltpu.VMEM((3, 16, 32, 128), BF),
            pltpu.VMEM((15, 32, 128), BF),
            pltpu.VMEM((15, 32, 128), BF),
            pltpu.VMEM((32, 128), F32),
            pltpu.VMEM((16, 32, 128), BF),
            pltpu.VMEM((8, 128), F32),
            pltpu.VMEM((8, 128), F32),
            pltpu.VMEM((8, 128), F32),
            pltpu.VMEM((3, 8, 128), F32),
            pltpu.VMEM((8, 128), F32),
            pltpu.VMEM((15, 8, 128), F32),
            pltpu.VMEM((8, 128), F32),
            pltpu.VMEM((8, 128, 256), BF),
            pltpu.VMEM((4, 128, 256), BF),
            pltpu.VMEM((8, 1024, 128), BF),
            pltpu.VMEM((256, 1024), F32),
        ]
        + sems,
        compiler_params=pltpu.CompilerParams(
            collective_id=0, has_side_effects=True, vmem_limit_bytes=56 * 1024 * 1024
        ),
        cost_estimate=pl.CostEstimate(flops=6 * 10**9, bytes_accessed=6 * 2**20, transcendentals=0),
    )(pool, dictionary, jnp.transpose(support), jnp.reshape(pick, (1, 256)))


def solution(mesh):
    placed = (P("frame", "vox"), P(None, "vox"), P(None, "vox"), P("frame"))
    return jax.shard_map(
        body,
        mesh=mesh,
        in_specs=placed,
        out_specs=(P("frame", None), P("frame", "vox")),
        check_vma=False,
    )
```

time: 749 us -> 84.1 us (0.11)
  waiting for transfers between devices: 451 us -> 0 us
  blocking collectives: 254 us -> 0 us
  Pallas kernels: 0 us -> 79.1 us
  between operations: 13.8 us -> 0.64 us
  matrix products: 13.1 us -> 0 us
  other arithmetic: 9.34 us -> 0 us
    psum x2 -> x0, waiting for transfers between devices: 418 us -> none  [the longest x1 332 us: body(): push = lax.psum(against(resid, masked), 'vox')]
    psum x1 -> x0, blocking collectives: 254 us -> none  [body(): corr, energy = lax.psum((corr_local, energy_local), 'vox')]
    pallas_call x0 -> x1, Pallas kernels: none -> 79.1 us  [body(): pl.pallas_call(kernel, out_shape=(jax.ShapeDtypeStruct((256, 1024), BF),...]
    reduce_scatter x1 -> x0, waiting for transfers between devices: 33.2 us -> none  [body(): lax.psum_scatter(lax.dot_general(codes, error, (((0,), (0,)), ((), ())),...]
    dot_general x3 -> x0, matrix products: 13.1 us -> none  [the longest x2 8.61 us: against(): lax.dot_general(left, right, (((1,), (1,)), ((), ())), preferred_element_...]
  transfers between devices with their start and end apart: 3 -> 0, of which waited for: 3 -> 0; matrix products, arithmetic and copies ran while one was open for 0% -> 0% of each run, Pallas kernels for 0% -> 0%
where the time goes in v1:
time: 84.1 us; the launch traced here: 83.9 us
  Pallas kernels  79.1 us (94%)
  local copies, waits for them, and re-layouts  4.17 us (5%)
    pallas_call x1, Pallas kernels, body(): pl.pallas_call(kernel, out_shape=(jax.ShapeDtypeStruct((256, 1024), BF),...  79.1 us
    unnamed x2, local copies, waits for them, and re-layouts  4.17 us

profile of v1, /device:TPU:1, one launch (start us, length us, event | category | flops | bytes accessed | tf_op | source)
XLA Modules:
  0.0 83.9 jit_solution(567518278517651920)
XLA Ops:
  0.6 79.1 %shard_map.59 = (bf16[256,1024]{1,0:T(8,128)(2,1)}, f32[256,1024]{1,0:T(8,128)}) custom-call(bf16[512,1024]{1,0:T(8,128)(2,1)} %pool.1, bf16[1024,1024]{1,0:T(8,128)(2,1)} %dico.1, s32[8,1024]{1,0:T(8,128)} %bitcast.2, s32[1,256]{1,0:T(1,128)} %bitcast.3), custom_call_target="tpu_custom_call" | custom-call | flops 6000000000 | bytes 6291456 | tf_op jit(solution)/shard_map/pallas_call | solution.py:237
  79.8 1.9 %copy.8 = bf16[256,1024]{1,0:T(8,128)(2,1)} copy(bf16[256,1024]{1,0:T(8,128)(2,1)} %get-tuple-element.4) | data formatting | bytes 1048576
  81.6 2.3 %copy.9 = f32[256,1024]{1,0:T(8,128)} copy(f32[256,1024]{1,0:T(8,128)} %get-tuple-element.5) | data formatting | bytes 2097152

commit v2 on v0

v2 whole, which is shorter than its diff:
```python
import jax
import jax.numpy as jnp
from jax import lax
from jax.experimental import pallas as pl
from jax.experimental.pallas import tpu as pltpu
from jax.sharding import PartitionSpec as P

MESH = pl.DeviceIdType.MESH
NX, NY, NZ = 4, 4, 16
FAR = (8, 7, 9, 6, 10, 5, 11, 4, 12, 3, 13, 2, 14, 1, 15, 0)
OFFS = (2, 1, 3)
SPLIT = 2
BF, F32 = jnp.bfloat16, jnp.float32


def shrink(value, limit):
    return jnp.where(value < 0, -1.0, 1.0) * jnp.maximum(jnp.abs(value) - limit, 0.0)


def mm_t(left, right):
    return lax.dot_general(left, right, (((1,), (1,)), ((), ())), preferred_element_type=F32)


def mm_0(left, right):
    return lax.dot_general(left, right, (((0,), (0,)), ((), ())), preferred_element_type=F32)


def column(row):
    return jnp.transpose(jnp.broadcast_to(row, (128, 128)))


def spread():
    block_of = lax.broadcasted_iota(jnp.int32, (8, 1024), 1) // 128
    return (block_of == lax.broadcasted_iota(jnp.int32, (8, 1024), 0)).astype(F32).astype(BF)


def gather(
    pool_in, dico_in, supt, pick, call, batch, masked,
    pool, dico, psend, pown, precv, xsend, xrecv, zsend, zrecv, zown, zall,
    e_own, e_core, e_x, e_xr, e_z, e_zr, e_step, steps, fall, gmat,
    l_pool, l_dico, s_b, r_b, s_p, r_p, s_ec, r_ec, s_ex, r_ex, s_ez, r_ez, s_x, r_x, s_z, r_z, s_a, r_a,
    s_f, r_f, s_g, r_g, s_cx, r_cx, s_cy, r_cy, s_dx, r_dx, s_dy, r_dy, s_cc, r_cc,
):
    y, v = lax.axis_index("frame"), lax.axis_index("vox")
    x, z, c = v // 32, (v // 2) % NZ, v % 2

    def dev(xx, yy, zz, cc):
        return (yy, (xx * NZ + zz) * 2 + cc)

    partner = dev(x, y, z, 1 - c)
    xs = [(x + i) % NX for i in OFFS]
    zs = [(z + o) % NZ for o in FAR]
    xpeer = [dev(xx, y, z, c) for xx in xs]
    xother = [dev(xx, y, z, 1 - c) for xx in xs]
    ypeer = [dev(x, (y + i) % NY, z, c) for i in OFFS]
    zpeer = [dev(x, y, zz, c) for zz in zs[:15]]
    sent = []

    def send(src, dst, ssem, rsem, to):
        copy = pltpu.make_async_remote_copy(
            src_ref=src, dst_ref=dst, send_sem=ssem, recv_sem=rsem, device_id=to, device_id_type=MESH
        )
        copy.start()
        sent.append(copy)
        return copy

    load_pool = pltpu.make_async_copy(pool_in, pool, l_pool)
    load_pool.start()
    load_dico = []
    for j in range(4):
        rows = pl.ds(256 * j, 256)
        load_dico.append(pltpu.make_async_copy(dico_in.at[rows], dico.at[rows], l_dico.at[j]))
        load_dico[j].start()
    barrier = pltpu.get_barrier_semaphore()
    everyone = [partner] + xpeer + xother + ypeer + zpeer
    for to in everyone:
        pl.semaphore_signal(barrier, inc=1, device_id=to, device_id_type=MESH)

    lane = lax.broadcasted_iota(jnp.int32, (128, 128), 1)
    mine = pl.multiple_of(y * 256, 256)
    hot = []
    for r in range(2):
        rows = column(pick[:, 128 * r : 128 * (r + 1)])
        hot.append(jnp.concatenate([(rows == lane + 128 * j).astype(F32).astype(BF) for j in range(4)], axis=1))
    hot = jnp.concatenate(hot, axis=0)
    load_pool.wait()
    batch[pl.ds(mine, 256), :] = jnp.dot(hot, pool[...], preferred_element_type=F32).astype(BF)

    wide = spread()
    for j in range(4):
        rows = slice(256 * j, 256 * (j + 1))
        kept = mm_0(supt[:, rows].astype(F32).astype(BF), wide).astype(BF)
        load_dico[j].wait()
        masked[rows, :] = dico[rows, :] * kept

    def products(half, g, out, kind):
        rows = pl.ds(pl.multiple_of(half * 512, 512), 512)
        right = (batch, masked)[g][pl.ds(mine, 256), :]
        value = mm_t(masked[rows, :], right).astype(kind)
        for xx in range(4):
            for zz in range(16):
                top = xx * 128 + 16 * (zz // 2)
                left = 128 * (zz % 2)
                out[g, xx * 16 + zz] = value[top : top + 16, left : left + 128]

    products(1 - c, 0, psend, BF)
    pl.semaphore_wait(barrier, len(everyone))
    pc = [send(psend.at[0], precv.at[0], s_p.at[0], r_p.at[0], partner)]
    products(1 - c, 1, psend, BF)
    pc.append(send(psend.at[1], precv.at[1], s_p.at[1], r_p.at[1], partner))
    own_batch = batch.at[pl.ds(mine, 256), :]
    b_copies = [send(own_batch, own_batch, s_b.at[k], r_b.at[k], ypeer[k]) for k in range(3)]
    products(c, 0, pown, F32)
    products(c, 1, pown, F32)

    pc[0].wait_recv()
    pc[1].wait_recv()
    xc = []
    for j in range(4):
        for k in range(3):
            for q in range(4):
                t = xs[k] * 16 + zs[4 * j + q]
                for g in range(2):
                    xsend[k, 4 * j + q, g] = (pown[g, t] + precv[g, t].astype(F32)).astype(BF)
            piece = pl.ds(4 * j, 4)
            xc.append(send(xsend.at[k, piece], xrecv.at[k, piece], s_x.at[k, j], r_x.at[k, j], xpeer[k]))

    for j in range(8):
        kept = masked[128 * j : 128 * (j + 1), :].astype(F32)
        part = jnp.zeros((128, 128), F32)
        for b in range(8):
            piece = kept[:, 128 * b : 128 * (b + 1)]
            part += piece * piece
        e_own[j : j + 1, :] = jnp.sum(jnp.transpose(part), axis=0, keepdims=True)
    ec = send(e_own, e_core, s_ec, r_ec, partner)

    zc = []
    for j in range(4):
        for k in range(3):
            xc[3 * j + k].wait_recv()
        for q in range(4):
            n = 4 * j + q
            t = x * 16 + zs[n]
            for g in range(2):
                total = pown[g, t] + precv[g, t].astype(F32)
                for k in range(3):
                    total += xrecv[k, n, g].astype(F32)
                if n < 15:
                    zsend[n, g] = total.astype(BF)
                else:
                    zown[g] = total
            if n < 15:
                zc.append(send(zsend.at[n], zrecv.at[n], s_z.at[n], r_z.at[n], zpeer[n]))
        if j == 0:
            ec.wait_recv()
            e_x[...] = e_own[...] + e_core[...]
            ex = [send(e_x, e_xr.at[k], s_ex.at[k], r_ex.at[k], xpeer[k]) for k in range(3)]
    for k in range(3):
        ex[k].wait_recv()
    e_z[...] = e_x[...] + e_xr[0] + e_xr[1] + e_xr[2]
    ez = [send(e_z, e_zr.at[n], s_ez.at[n], r_ez.at[n], zpeer[n]) for n in range(15)]
    total = zown[...]
    for n in reversed(range(15)):
        zc[n].wait_recv()
        total += zrecv[n].astype(F32)
    zall[15] = total.astype(BF)
    za = [send(zall.at[15], zall.at[n], s_a.at[n], r_a.at[n], zpeer[n]) for n in range(15)]

    for n in reversed(range(15)):
        ez[n].wait_recv()
    energy = e_z[...]
    for n in range(15):
        energy += e_zr[n]
    e_step[...] = 1.0 / (energy + 1e-05)
    block = c * 4 + x
    steps[...] = column(e_step[pl.ds(block, 1), :])

    fc, gc = [], []
    size = 16 // SPLIT
    for j in reversed(range(SPLIT)):
        for n in reversed(range(size * j, size * (j + 1))):
            if n < 15:
                za[n].wait_recv()
            came = (z + NZ - FAR[n]) % NZ
            step = steps[pl.ds(pl.multiple_of(16 * (came // 2), 16), 16), :]
            fall[block, n] = shrink(zall[n, 0].astype(F32) * step, 0.3 * step).astype(BF)
            gmat[y, n] = zall[n, 1]
        piece = pl.ds(size * j, size)
        own_f, own_g = fall.at[block, piece], gmat.at[y, piece]
        for k, to in enumerate(xpeer + xother + [partner]):
            fc.append(send(own_f, own_f, s_f.at[k, j], r_f.at[k, j], to))
        for k in range(3):
            gc.append(send(own_g, own_g, s_g.at[k, j], r_g.at[k, j], ypeer[k]))
    for copy in gc + fc:
        copy.wait_recv()

    def at(row, half):
        o = (z + NZ - 2 * row - half) % NZ
        return jnp.where(o >= 8, 2 * o - 16, 15 - 2 * o)

    def matrix(tiles):
        sides = [jnp.concatenate([tiles(at(row, half)) for row in range(8)], axis=0) for half in range(2)]
        return jnp.concatenate(sides, axis=1)

    push = -matrix(lambda n: zall[n, 0]).astype(F32)
    for g in range(4):
        left = matrix(lambda n: gmat[g, n])
        right = jnp.concatenate([matrix(lambda n: fall[2 * g + b, n]) for b in range(2)], axis=0)
        push += jnp.dot(left, right, preferred_element_type=F32)
    step = jnp.concatenate([steps[...], steps[...]], axis=1)
    first = matrix(lambda n: fall[block, n]).astype(F32)
    codes = shrink(first - step * push, 0.3 * step)
    call[block, pl.ds(mine, 256), :] = jnp.transpose(codes).astype(BF)

    def slot(b, yy, half):
        return call.at[b, pl.ds(pl.multiple_of(yy * 256 + half * 128, 128), 128), :]

    def across(copies, half, over_x):
        ref = slot(block, y, half)
        for k in range(3):
            sems = (s_cx, r_cx) if over_x else (s_cy, r_cy)
            to = xpeer[k] if over_x else ypeer[k]
            copies.append(send(ref, ref, sems[0].at[half, k], sems[1].at[half, k], to))

    x0, x1, y0, y1 = [], [], [], []
    across(x0, 0, True)
    across(y1, 1, False)
    across(x1, 1, True)
    across(y0, 0, False)
    dx, dy = {}, {}
    for k in (1, 2, 0):
        x0[k].wait_recv()
        ref = slot(c * 4 + (x + NX - OFFS[k]) % NX, y, 0)
        for m in range(3):
            dy[k, m] = send(ref, ref, s_dy.at[k, m], r_dy.at[k, m], ypeer[m])
        y1[k].wait_recv()
        ref = slot(block, (y + NY - OFFS[k]) % NY, 1)
        for m in range(3):
            dx[k, m] = send(ref, ref, s_dx.at[k, m], r_dx.at[k, m], xpeer[m])
    cc = []

    def to_partner(yy, half, n):
        ref = call.at[pl.ds(c * 4, 4), pl.ds(pl.multiple_of(yy * 256 + half * 128, 128), 128), :]
        cc.append(send(ref, ref, s_cc.at[n], r_cc.at[n], partner))

    to_partner(y, 0, 0)
    for k in range(3):
        x1[k].wait_recv()
    to_partner(y, 1, 1)
    for m in (1, 2, 0):
        yy = (y + NY - OFFS[m]) % NY
        y0[m].wait_recv()
        for k in range(3):
            dy[k, m].wait_recv()
        to_partner(yy, 0, 2 + 2 * m)
        for k in range(3):
            dx[m, k].wait_recv()
        to_partner(yy, 1, 3 + 2 * m)
    for copy in cc + b_copies:
        copy.wait_recv()
    for copy in sent:
        copy.wait_send()


def finish(call, batch, masked, supt, codes_out, grad_out, own):
    y = lax.axis_index("frame")

    @pl.when(pl.program_id(0) == 0)
    def _():
        rows = pl.ds(pl.multiple_of(y * 256, 256), 256)
        codes_out[...] = jnp.concatenate([call[b, rows, :] for b in range(8)], axis=1)
        for h in range(2):
            own[128 * h : 128 * (h + 1), :] = jnp.transpose(call[2 * y + h])

    total = jnp.zeros((256, 256), F32)
    for half in range(2):
        rows = slice(512 * half, 512 * (half + 1))
        codes = jnp.concatenate([call[b, rows, :] for b in range(8)], axis=1)
        rest = jnp.dot(codes, masked[...], preferred_element_type=F32) - batch[rows, :].astype(F32)
        total += jnp.dot(own[:, rows], rest.astype(BF), preferred_element_type=F32)
    first = pl.program_id(0) * 2
    sup = supt[:, pl.ds(pl.multiple_of(y * 256, 256), 256)].astype(F32).astype(BF)
    place = lax.broadcasted_iota(jnp.int32, (8, 256), 1) // 128 + first
    pick = (place == lax.broadcasted_iota(jnp.int32, (8, 256), 0)).astype(F32).astype(BF)
    grad_out[...] = total * mm_0(sup, pick) * (1.0 / 1024)


def body(pool, dictionary, support, pick):
    dma = pltpu.SemaphoreType.DMA
    sems = [dma(()), dma((4,))]
    for shape in ((3,), (2,), (), (3,), (15,), (3, 4), (15,), (15,), (7, SPLIT), (3, SPLIT), (2, 3), (2, 3), (3, 3), (3, 3), (8,)):
        sems += [dma(shape), dma(shape)]
    vmem = pl.BlockSpec(memory_space=pltpu.VMEM)
    hbm = pl.BlockSpec(memory_space=pltpu.HBM)
    supt = jnp.transpose(support)
    call, batch, masked = pl.pallas_call(
        gather,
        out_shape=(
            jax.ShapeDtypeStruct((8, 1024, 128), BF),
            jax.ShapeDtypeStruct((1024, 1024), BF),
            jax.ShapeDtypeStruct((1024, 1024), BF),
        ),
        in_specs=[hbm, hbm, vmem, vmem],
        out_specs=(vmem, vmem, vmem),
        scratch_shapes=[
            pltpu.VMEM((512, 1024), BF),
            pltpu.VMEM((1024, 1024), BF),
            pltpu.VMEM((2, 64, 16, 128), BF),
            pltpu.VMEM((2, 64, 16, 128), F32),
            pltpu.VMEM((2, 64, 16, 128), BF),
            pltpu.VMEM((3, 16, 2, 16, 128), BF),
            pltpu.VMEM((3, 16, 2, 16, 128), BF),
            pltpu.VMEM((15, 2, 16, 128), BF),
            pltpu.VMEM((15, 2, 16, 128), BF),
            pltpu.VMEM((2, 16, 128), F32),
            pltpu.VMEM((16, 2, 16, 128), BF),
            pltpu.VMEM((8, 128), F32),
            pltpu.VMEM((8, 128), F32),
            pltpu.VMEM((8, 128), F32),
            pltpu.VMEM((3, 8, 128), F32),
            pltpu.VMEM((8, 128), F32),
            pltpu.VMEM((15, 8, 128), F32),
            pltpu.VMEM((8, 128), F32),
            pltpu.VMEM((128, 128), F32),
            pltpu.VMEM((8, 16, 16, 128), BF),
            pltpu.VMEM((4, 16, 16, 128), BF),
        ]
        + sems,
        compiler_params=pltpu.CompilerParams(
            collective_id=0, has_side_effects=True, vmem_limit_bytes=28 * 1024 * 1024
        ),
        cost_estimate=pl.CostEstimate(flops=3 * 10**9, bytes_accessed=6 * 2**20, transcendentals=0),
        name="gather",
    )(pool, dictionary, supt, jnp.reshape(pick, (1, 256)))
    return pl.pallas_call(
        finish,
        grid=(4,),
        out_shape=(jax.ShapeDtypeStruct((256, 1024), BF), jax.ShapeDtypeStruct((256, 1024), F32)),
        in_specs=[
            pl.BlockSpec((8, 1024, 128), lambda n: (0, 0, 0)),
            pl.BlockSpec((1024, 256), lambda n: (0, n)),
            pl.BlockSpec((1024, 256), lambda n: (0, n)),
            pl.BlockSpec((8, 1024), lambda n: (0, 0)),
        ],
        out_specs=(
            pl.BlockSpec((256, 1024), lambda n: (0, 0)),
            pl.BlockSpec((256, 256), lambda n: (0, n)),
        ),
        scratch_shapes=[pltpu.VMEM((256, 1024), BF)],
        compiler_params=pltpu.CompilerParams(vmem_limit_bytes=28 * 1024 * 1024),
        cost_estimate=pl.CostEstimate(flops=3 * 10**9, bytes_accessed=6 * 2**20, transcendentals=0),
        name="finish",
    )(call, batch, masked, supt)


def solution(mesh):
    placed = (P("frame", "vox"), P(None, "vox"), P(None, "vox"), P("frame"))
    return jax.shard_map(
        body,
        mesh=mesh,
        in_specs=placed,
        out_specs=(P("frame", None), P("frame", "vox")),
        check_vma=False,
    )
```

time: 749 us -> 74.8 us (0.10)
  waiting for transfers between devices: 451 us -> 0 us
  blocking collectives: 254 us -> 0 us
  Pallas kernels: 0 us -> 69.5 us
  between operations: 13.8 us -> 0.66 us
  matrix products: 13.1 us -> 0 us
  other arithmetic: 9.34 us -> 0 us
    psum x2 -> x0, waiting for transfers between devices: 418 us -> none  [the longest x1 332 us: body(): push = lax.psum(against(resid, masked), 'vox')]
    psum x1 -> x0, blocking collectives: 254 us -> none  [body(): corr, energy = lax.psum((corr_local, energy_local), 'vox')]
    pallas_call x0 -> x2, Pallas kernels: none -> 69.5 us  [the longest x1 63.3 us: body(): pl.pallas_call(gather, out_shape=(jax.ShapeDtypeStruct((8, 1024, 128), BF...]
    reduce_scatter x1 -> x0, waiting for transfers between devices: 33.2 us -> none  [body(): lax.psum_scatter(lax.dot_general(codes, error, (((0,), (0,)), ((), ())),...]
    dot_general x3 -> x0, matrix products: 13.1 us -> none  [the longest x2 8.61 us: against(): lax.dot_general(left, right, (((1,), (1,)), ((), ())), preferred_element_...]
  transfers between devices with their start and end apart: 3 -> 0, of which waited for: 3 -> 0; matrix products, arithmetic and copies ran while one was open for 0% -> 0% of each run, Pallas kernels for 0% -> 0%
where the time goes in v2:
time: 74.8 us; the launch traced here: 74.4 us
  Pallas kernels  69.5 us (93%)
  local copies, waits for them, and re-layouts  4.25 us (6%)
    pallas_call x1, Pallas kernels, body(): pl.pallas_call(gather, out_shape=(jax.ShapeDtypeStruct((8, 1024, 128), BF...  63.3 us
    pallas_call x1, Pallas kernels, body(): pl.pallas_call(finish, grid=(4,), out_shape=(jax.ShapeDtypeStruct((256, 1...  6.22 us
    unnamed x10, local copies, waits for them, and re-layouts  4.25 us

profile of v2, /device:TPU:1, one launch (start us, length us, event | category | flops | bytes accessed | tf_op | source)
XLA Modules:
  0.0 74.4 jit_solution(12597852261456908119)
XLA Ops:
  0.6 0.0 copy-start
  0.6 1.6 %copy-done = bf16[1024,1024]{1,0:T(8,128)(2,1)S(1)} copy-done((bf16[1024,1024]{1,0:T(8,128)(2,1)S(1)}, bf16[1024,1024]{1,0:T(8,128)(2,1)}, u32[]{:S(2)}) %copy-start) | copy-done | bytes 2097176
  2.2 0.0 copy-start.1
  2.2 1.2 %copy-done.1 = bf16[512,1024]{1,0:T(8,128)(2,1)S(1)} copy-done((bf16[512,1024]{1,0:T(8,128)(2,1)S(1)}, bf16[512,1024]{1,0:T(8,128)(2,1)}, u32[]{:S(2)}) %copy-start.1) | copy-done | bytes 1048600
  3.4 0.0 copy-start.2
  3.5 0.8 %copy-done.2 = s32[1024,8]{0,1:T(8,128)S(1)} copy-done((s32[1024,8]{0,1:T(8,128)S(1)}, s32[1024,8]{0,1:T(8,128)}, u32[]{:S(2)}) %copy-start.2) | copy-done | bytes 32792
  4.2 0.0 copy-start.4
  4.2 0.7 copy-done.4
  4.9 0.0 copy-start.3
  4.9 63.3 %gather.1 = (bf16[8,1024,128]{2,1,0:T(8,128)(2,1)S(1)}, bf16[1024,1024]{1,0:T(8,128)(2,1)S(1)}, bf16[1024,1024]{1,0:T(8,128)(2,1)S(1)}) custom-call(bf16[512,1024]{1,0:T(8,128)(2,1)S(1)} %copy-done.1, bf16[1024,1024]{1,0:T(8,128)(2,1)S(1)} %copy-done, s32[8,1024]{1,0:T(8,128)S(1)} %bitcast.2, s32[1,256]{1,0:T(1,128)S(1)} %bitcast.4), custom_call_target="tpu_custom_call" | custom-call | flops 3000000000 | bytes 6291456 | tf_op jit(solution)/shard_map/gather/pallas_call | solution.py:296
  68.2 0.0 copy-done.3
  68.2 6.2 %finish.1 = (bf16[256,1024]{1,0:T(8,128)(2,1)}, f32[256,1024]{1,0:T(8,128)}) custom-call(bf16[8,1024,128]{2,1,0:T(8,128)(2,1)S(1)} %get-tuple-element.5.call, bf16[1024,1024]{1,0:T(8,128)(2,1)S(1)} %get-tuple-element.6.batch, bf16[1024,1024]{1,0:T(8,128)(2,1)S(1)} %get-tuple-element.7.masked, s32[8,1024]{1,0:T(8,128)S(1)} %bitcast.3), custom_call_target="tpu_custom_call" | custom-call | flops 3000000000 | bytes 6291456 | tf_op jit(solution)/shard_map/finish/pallas_call | solution.py:335
Async XLA Ops:
  0.6 1.6 %copy-start = (bf16[1024,1024]{1,0:T(8,128)(2,1)S(1)}, bf16[1024,1024]{1,0:T(8,128)(2,1)}, u32[]{:S(2)}) copy-start(bf16[1024,1024]{1,0:T(8,128)(2,1)} %dico_in.1) | copy-start | bytes 6291460
  2.2 1.2 %copy-start.1 = (bf16[512,1024]{1,0:T(8,128)(2,1)S(1)}, bf16[512,1024]{1,0:T(8,128)(2,1)}, u32[]{:S(2)}) copy-start(bf16[512,1024]{1,0:T(8,128)(2,1)} %pool_in.1) | copy-start | bytes 3145732
  3.4 0.8 %copy-start.2 = (s32[1024,8]{0,1:T(8,128)S(1)}, s32[1024,8]{0,1:T(8,128)}, u32[]{:S(2)}) copy-start(s32[1024,8]{0,1:T(8,128)} %param.6) | copy-start | bytes 98308
  4.2 0.7 copy-start.4
  4.9 63.3 %copy-start.3 = (s32[1024,8]{0,1:T(8,128)S(1)}, s32[1024,8]{0,1:T(8,128)}, u32[]{:S(2)}) copy-start(s32[1024,8]{0,1:T(8,128)} %param.6) | copy-start | bytes 98308

commit v3 on v2

v3 whole, which is shorter than its diff:
```python
import jax
import jax.numpy as jnp
from jax import lax
from jax.experimental import pallas as pl
from jax.experimental.pallas import tpu as pltpu
from jax.sharding import PartitionSpec as P

MESH = pl.DeviceIdType.MESH
NX, NY, NZ = 4, 4, 16
FAR = (8, 7, 9, 6, 10, 5, 11, 4, 12, 3, 13, 2, 14, 1, 15, 0)
OFFS = (2, 1, 3)
SPLIT = 2
BF, F32 = jnp.bfloat16, jnp.float32


def shrink(value, limit):
    return jnp.where(value < 0, -1.0, 1.0) * jnp.maximum(jnp.abs(value) - limit, 0.0)


def mm_t(left, right):
    return lax.dot_general(left, right, (((1,), (1,)), ((), ())), preferred_element_type=F32)


def mm_0(left, right):
    return lax.dot_general(left, right, (((0,), (0,)), ((), ())), preferred_element_type=F32)


def column(row):
    return jnp.transpose(jnp.broadcast_to(row, (128, 128)))


def spread():
    block_of = lax.broadcasted_iota(jnp.int32, (8, 1024), 1) // 128
    return (block_of == lax.broadcasted_iota(jnp.int32, (8, 1024), 0)).astype(F32).astype(BF)


def gather(
    pool_in, dico_in, supt_in, pick_in, codes_out, total_out,
    pool, dico, supt, pick, call, batch, masked, group_out, total, psend, pown, precv, xsend, xrecv, zsend, zrecv, zown, zall,
    e_own, e_core, e_x, e_xr, e_z, e_zr, e_step, steps, fall, gmat,
    l_pool, l_dico, l_small, l_codes, l_total,
    s_b, r_b, s_p, r_p, s_e, r_e, s_x, r_x, s_z, r_z, s_a, r_a, s_f, r_f, s_g, r_g, s_c, s_cc, r_a0, r_all, r_cc,
):
    y, v = lax.axis_index("frame"), lax.axis_index("vox")
    x, z, c = v // 32, (v // 2) % NZ, v % 2

    def dev(xx, yy, zz, cc):
        return (yy, (xx * NZ + zz) * 2 + cc)

    partner = dev(x, y, z, 1 - c)
    xs = [(x + i) % NX for i in OFFS]
    zs = [(z + o) % NZ for o in FAR]
    xpeer = [dev(xx, y, z, c) for xx in xs]
    xother = [dev(xx, y, z, 1 - c) for xx in xs]
    ypeer = [dev(x, (y + i) % NY, z, c) for i in OFFS]
    zpeer = [dev(x, y, zz, c) for zz in zs[:15]]

    def send(src, dst, ssem, rsem, to):
        pltpu.make_async_remote_copy(
            src_ref=src, dst_ref=dst, send_sem=ssem, recv_sem=rsem, device_id=to, device_id_type=MESH
        ).start()

    def arrived(ref, sem):
        pltpu.make_async_copy(ref, ref, sem).wait()


    load_pick = pltpu.make_async_copy(pick_in, pick, l_small.at[0])
    load_pick.start()
    load_pool = pltpu.make_async_copy(pool_in, pool, l_pool)
    load_pool.start()
    load_supt = pltpu.make_async_copy(supt_in, supt, l_small.at[1])
    load_supt.start()
    load_dico = []
    for j in range(4):
        rows = pl.ds(256 * j, 256)
        load_dico.append(pltpu.make_async_copy(dico_in.at[rows], dico.at[rows], l_dico.at[j]))
        load_dico[j].start()
    barrier = pltpu.get_barrier_semaphore()
    everyone = [partner] + xpeer + xother + ypeer + zpeer
    for to in everyone:
        pl.semaphore_signal(barrier, inc=1, device_id=to, device_id_type=MESH)

    lane = lax.broadcasted_iota(jnp.int32, (128, 128), 1)
    mine = pl.multiple_of(y * 256, 256)
    hot = []
    load_pick.wait()
    for r in range(2):
        rows = column(pick[:, 128 * r : 128 * (r + 1)])
        hot.append(jnp.concatenate([(rows == lane + 128 * j).astype(F32).astype(BF) for j in range(4)], axis=1))
    hot = jnp.concatenate(hot, axis=0)
    load_pool.wait()
    batch[pl.ds(mine, 256), :] = jnp.dot(hot, pool[...], preferred_element_type=F32).astype(BF)

    wide = spread()
    load_supt.wait()
    for j in range(4):
        rows = slice(256 * j, 256 * (j + 1))
        kept = mm_0(supt[:, rows].astype(F32).astype(BF), wide).astype(BF)
        load_dico[j].wait()
        masked[rows, :] = dico[rows, :] * kept

    def products(half, g, out, kind):
        rows = pl.ds(pl.multiple_of(half * 512, 512), 512)
        right = (batch, masked)[g][pl.ds(mine, 256), :]
        value = mm_t(masked[rows, :], right).astype(kind)
        for xx in range(4):
            for zz in range(16):
                top = xx * 128 + 16 * (zz // 2)
                left = 128 * (zz % 2)
                out[g, xx * 16 + zz] = value[top : top + 16, left : left + 128]

    products(1 - c, 0, psend, BF)
    products(1 - c, 1, psend, BF)
    pl.semaphore_wait(barrier, len(everyone))
    send(psend, precv, s_p, r_p, partner)
    own_batch = batch.at[pl.ds(mine, 256), :]
    for k in range(3):
        send(own_batch, own_batch, s_b, r_b.at[k], ypeer[k])
    products(c, 0, pown, F32)
    products(c, 1, pown, F32)

    arrived(precv, r_p)
    for j in range(4):
        for k in range(3):
            for q in range(4):
                t = xs[k] * 16 + zs[4 * j + q]
                for g in range(2):
                    xsend[k, 4 * j + q, g] = (pown[g, t] + precv[g, t].astype(F32)).astype(BF)
            piece = pl.ds(4 * j, 4)
            send(xsend.at[k, piece], xrecv.at[k, piece], s_x, r_x.at[j], xpeer[k])

    for j in range(8):
        kept = masked[128 * j : 128 * (j + 1), :].astype(F32)
        part = jnp.zeros((128, 128), F32)
        for b in range(8):
            piece = kept[:, 128 * b : 128 * (b + 1)]
            part += piece * piece
        e_own[j : j + 1, :] = jnp.sum(jnp.transpose(part), axis=0, keepdims=True)
    send(e_own, e_core, s_e.at[0], r_e.at[0], partner)

    for j in range(4):
        arrived(xrecv.at[:, 4 * j : 4 * j + 4], r_x.at[j])
        for q in range(4):
            n = 4 * j + q
            t = x * 16 + zs[n]
            for g in range(2):
                added = pown[g, t] + precv[g, t].astype(F32)
                for k in range(3):
                    added += xrecv[k, n, g].astype(F32)
                if n < 15:
                    zsend[n, g] = added.astype(BF)
                else:
                    zown[g] = added
            if n < 15:
                send(zsend.at[n], zrecv.at[n], s_z, r_z, zpeer[n])
        if j == 0:
            arrived(e_core, r_e.at[0])
            e_x[...] = e_own[...] + e_core[...]
            for k in range(3):
                send(e_x, e_xr.at[k], s_e.at[1], r_e.at[1], xpeer[k])
    arrived(e_xr, r_e.at[1])
    e_z[...] = e_x[...] + e_xr[0] + e_xr[1] + e_xr[2]
    for n in range(15):
        send(e_z, e_zr.at[n], s_e.at[2], r_e.at[2], zpeer[n])
    arrived(zrecv, r_z)
    added = zown[...]
    for n in range(15):
        added += zrecv[n].astype(F32)
    zall[15] = added.astype(BF)
    size = 16 // SPLIT
    for n in range(15):
        send(zall.at[15], zall.at[n], s_a, r_a.at[n // size], zpeer[n])

    arrived(e_zr, r_e.at[2])
    energy = e_z[...]
    for n in range(15):
        energy += e_zr[n]
    e_step[...] = 1.0 / (energy + 1e-05)
    block = c * 4 + x
    steps[...] = column(e_step[pl.ds(block, 1), :])

    for j in reversed(range(SPLIT)):
        arrived(zall.at[size * j : min(size * (j + 1), 15)], r_a.at[j])
        for n in reversed(range(size * j, size * (j + 1))):
            came = (z + NZ - FAR[n]) % NZ
            step = steps[pl.ds(pl.multiple_of(16 * (came // 2), 16), 16), :]
            fall[block, n] = shrink(zall[n, 0].astype(F32) * step, 0.3 * step).astype(BF)
            gmat[y, n] = zall[n, 1]
        piece = pl.ds(size * j, size)
        own_f, own_g = fall.at[block, piece], gmat.at[y, piece]
        for to in xpeer + xother + [partner]:
            send(own_f, own_f, s_f, r_f, to)
        for k in range(3):
            send(own_g, own_g, s_g, r_g, ypeer[k])
    arrived(fall.at[0:7], r_f)
    arrived(gmat.at[0:3], r_g)

    def at(row, half):
        o = (z + NZ - 2 * row - half) % NZ
        return jnp.where(o >= 8, 2 * o - 16, 15 - 2 * o)

    def matrix(tiles):
        sides = [jnp.concatenate([tiles(at(row, half)) for row in range(8)], axis=0) for half in range(2)]
        return jnp.concatenate(sides, axis=1)

    push = -matrix(lambda n: zall[n, 0]).astype(F32)
    for g in range(4):
        left = matrix(lambda n: gmat[g, n])
        right = jnp.concatenate([matrix(lambda n: fall[2 * g + b, n]) for b in range(2)], axis=0)
        push += jnp.dot(left, right, preferred_element_type=F32)
    step = jnp.concatenate([steps[...], steps[...]], axis=1)
    first = matrix(lambda n: fall[block, n]).astype(F32)
    codes = shrink(first - step * push, 0.3 * step)
    call[block, pl.ds(mine, 256), :] = jnp.transpose(codes).astype(BF)

    def slot(b, yy, half):
        return call.at[b, pl.ds(pl.multiple_of(yy * 256 + half * 128, 128), 128), :]

    def across(half, over_x, sems):
        ref = slot(block, y, half)
        for k in range(3):
            send(ref, ref, s_c, sems[k], (xpeer if over_x else ypeer)[k])

    across(0, True, [r_a0.at[0, k] for k in range(3)])
    across(1, False, [r_a0.at[1, k] for k in range(3)])
    across(1, True, [r_all.at[0, 1]] * 3)
    across(0, False, [r_all.at[1 + k, 0] for k in range(3)])
    third = call.at[0, 0:128, :]
    for k in (1, 2, 0):
        arrived(third, r_a0.at[0, k])
        ref = slot(c * 4 + (x + NX - OFFS[k]) % NX, y, 0)
        for m in range(3):
            send(ref, ref, s_c, r_all.at[1 + m, 0], ypeer[m])
        arrived(third, r_a0.at[1, k])
        ref = slot(block, (y + NY - OFFS[k]) % NY, 1)
        for m in range(3):
            send(ref, ref, s_c, r_all.at[1 + k, 1], xpeer[m])

    def to_partner(yy, half, turn):
        ref = call.at[pl.ds(c * 4, 4), pl.ds(pl.multiple_of(yy * 256 + half * 128, 128), 128), :]
        send(ref, ref, s_cc, r_cc.at[turn], partner)

    def pass_on(turn):
        yy, m = groups[turn]
        if m is None:
            to_partner(yy, 0, turn)
            arrived(call.at[0:3, 0:128, :], r_all.at[0, 1])
            to_partner(yy, 1, turn)
        else:
            arrived(call.at[0:4, 0:128, :], r_all.at[1 + m, 0])
            to_partner(yy, 0, turn)
            arrived(call.at[0:3, 0:128, :], r_all.at[1 + m, 1])
            to_partner(yy, 1, turn)

    def products_of(turn):
        yy, m = groups[turn]
        arrived(call.at[0:4, 0:256, :], r_cc.at[turn])
        if m is not None:
            arrived(own_batch, r_b.at[m])
        rows = pl.ds(pl.multiple_of(yy * 256, 256), 256)
        group = jnp.concatenate([call[b, rows, :] for b in range(8)], axis=1)
        if m is None:
            group_out[...] = group
            write_codes.start()
        own = jnp.concatenate([jnp.transpose(call[2 * y + h, rows, :]) for h in range(2)], axis=0)
        for n in range(2):
            cols = slice(512 * n, 512 * (n + 1))
            rest = jnp.dot(group, masked[:, cols], preferred_element_type=F32) - batch[rows, cols].astype(F32)
            part = jnp.dot(own, rest.astype(BF), preferred_element_type=F32)
            if turn == 0:
                total[:, cols] = part
            else:
                total[:, cols] += part
            if turn == 3:
                write_total[n].start()

    groups = [(y, None)] + [((y + NY - OFFS[m]) % NY, m) for m in (1, 2, 0)]
    write_codes = pltpu.make_async_copy(group_out, codes_out, l_codes)
    write_total = []
    for n in range(2):
        cols = slice(512 * n, 512 * (n + 1))
        write_total.append(pltpu.make_async_copy(total.at[:, cols], total_out.at[:, cols], l_total.at[n]))
    pass_on(0)
    products_of(0)
    pass_on(1)
    pass_on(2)
    products_of(1)
    pass_on(3)
    products_of(2)
    products_of(3)
    write_codes.wait()
    for n in range(2):
        write_total[n].wait()
    for ref, sem in (
        (batch.at[0:768, :], s_b),
        (psend, s_p),
        (e_own, s_e.at[0]),
        (e_xr, s_e.at[1]),
        (e_zr, s_e.at[2]),
        (xsend, s_x),
        (zsend, s_z),
        (zall.at[0:15], s_a),
        (fall.at[0:7], s_f),
        (gmat.at[0:3], s_g),
        (call.at[0:5, 0:768, :], s_c),
        (call.at[0:4], s_cc),
    ):
        arrived(ref, sem)


def finish(codes, total, supt, codes_out, grad_out):
    y = lax.axis_index("frame")
    codes_out[...] = codes[...]
    sup = supt[:, pl.ds(pl.multiple_of(y * 256, 256), 256)].astype(F32).astype(BF)
    first = pl.program_id(0) * 4
    place = lax.broadcasted_iota(jnp.int32, (8, 512), 1) // 128 + first
    pick = (place == lax.broadcasted_iota(jnp.int32, (8, 512), 0)).astype(F32).astype(BF)
    grad_out[...] = total[...] * mm_0(sup, pick) * (1.0 / 1024)


def body(pool, dictionary, support, pick):
    dma = pltpu.SemaphoreType.DMA
    sems = [dma(()), dma((4,)), dma((2,)), dma(()), dma((2,))]
    for shape in ((), (3,), (), (), (3,), (3,), (), (4,), (), (), (), (SPLIT,), (), (), (), (), (), (), (2, 3), (4, 2), (4,)):
        sems.append(dma(shape))
    hbm = pl.BlockSpec(memory_space=pl.ANY)
    supt = jnp.transpose(support)
    codes, total = pl.pallas_call(
        gather,
        out_shape=(jax.ShapeDtypeStruct((256, 1024), BF), jax.ShapeDtypeStruct((256, 1024), F32)),
        in_specs=[hbm] * 4,
        out_specs=(hbm, hbm),
        scratch_shapes=[
            pltpu.VMEM((512, 1024), BF),
            pltpu.VMEM((1024, 1024), BF),
            pltpu.VMEM((8, 1024), jnp.int32),
            pltpu.VMEM((1, 256), jnp.int32),
            pltpu.VMEM((8, 1024, 128), BF),
            pltpu.VMEM((1024, 1024), BF),
            pltpu.VMEM((1024, 1024), BF),
            pltpu.VMEM((256, 1024), BF),
            pltpu.VMEM((256, 1024), F32),
            pltpu.VMEM((2, 64, 16, 128), BF),
            pltpu.VMEM((2, 64, 16, 128), F32),
            pltpu.VMEM((2, 64, 16, 128), BF),
            pltpu.VMEM((3, 16, 2, 16, 128), BF),
            pltpu.VMEM((3, 16, 2, 16, 128), BF),
            pltpu.VMEM((15, 2, 16, 128), BF),
            pltpu.VMEM((15, 2, 16, 128), BF),
            pltpu.VMEM((2, 16, 128), F32),
            pltpu.VMEM((16, 2, 16, 128), BF),
            pltpu.VMEM((8, 128), F32),
            pltpu.VMEM((8, 128), F32),
            pltpu.VMEM((8, 128), F32),
            pltpu.VMEM((3, 8, 128), F32),
            pltpu.VMEM((8, 128), F32),
            pltpu.VMEM((15, 8, 128), F32),
            pltpu.VMEM((8, 128), F32),
            pltpu.VMEM((128, 128), F32),
            pltpu.VMEM((8, 16, 16, 128), BF),
            pltpu.VMEM((4, 16, 16, 128), BF),
        ]
        + sems,
        compiler_params=pltpu.CompilerParams(
            collective_id=0, has_side_effects=True, vmem_limit_bytes=56 * 1024 * 1024
        ),
        cost_estimate=pl.CostEstimate(flops=3 * 10**9, bytes_accessed=6 * 2**20, transcendentals=0),
        name="gather",
    )(pool, dictionary, supt, jnp.reshape(pick, (1, 256)))
    return pl.pallas_call(
        finish,
        grid=(2,),
        out_shape=(jax.ShapeDtypeStruct((256, 1024), BF), jax.ShapeDtypeStruct((256, 1024), F32)),
        in_specs=[
            pl.BlockSpec((256, 512), lambda n: (0, n)),
            pl.BlockSpec((256, 512), lambda n: (0, n)),
            pl.BlockSpec((8, 1024), lambda n: (0, 0)),
        ],
        out_specs=(
            pl.BlockSpec((256, 512), lambda n: (0, n)),
            pl.BlockSpec((256, 512), lambda n: (0, n)),
        ),
        compiler_params=pltpu.CompilerParams(vmem_limit_bytes=56 * 1024 * 1024),
        cost_estimate=pl.CostEstimate(flops=10**7, bytes_accessed=3 * 2**20, transcendentals=0),
        name="finish",
    )(codes, total, supt)


def solution(mesh):
    placed = (P("frame", "vox"), P(None, "vox"), P(None, "vox"), P("frame"))
    return jax.shard_map(
        body,
        mesh=mesh,
        in_specs=placed,
        out_specs=(P("frame", None), P("frame", "vox")),
        check_vma=False,
    )
```

time: 74.8 us -> 69 us (0.922)
  local copies, waits for them, and re-layouts: 4.25 us -> 0 us
  Pallas kernels: 69.5 us -> 68.2 us
    unnamed x10 -> x0, local copies, waits for them, and re-layouts: 4.25 us -> none
    pallas_call x2, Pallas kernels: 69.5 us -> 68.2 us  [the longest x1 65.7 us: body(): pl.pallas_call(gather, out_shape=(jax.ShapeDtypeStruct((256, 1024), BF),...]
where the time goes in v3:
time: 69 us; the launch traced here: 68.9 us
  Pallas kernels  68.2 us (99%)
    pallas_call x1, Pallas kernels, body(): pl.pallas_call(gather, out_shape=(jax.ShapeDtypeStruct((256, 1024), BF),...  65.7 us
    pallas_call x1, Pallas kernels, body(): pl.pallas_call(finish, grid=(2,), out_shape=(jax.ShapeDtypeStruct((256, 1...  2.52 us

profile of v3, /device:TPU:1, one launch (start us, length us, event | category | flops | bytes accessed | tf_op | source)
XLA Modules:
  0.0 68.9 jit_solution(14735469784765175487)
XLA Ops:
  0.6 65.7 %gather.1 = (bf16[256,1024]{1,0:T(8,128)(2,1)}, f32[256,1024]{1,0:T(8,128)}) custom-call(bf16[512,1024]{1,0:T(8,128)(2,1)} %pool_in.1, bf16[1024,1024]{1,0:T(8,128)(2,1)} %dico_in.1, s32[8,1024]{1,0:T(8,128)} %bitcast.2, s32[1,256]{1,0:T(1,128)} %bitcast.4), custom_call_target="tpu_custom_call" | custom-call | flops 3000000000 | bytes 6291456 | tf_op jit(solution)/shard_map/gather/pallas_call | solution.py:328
  66.3 2.5 %finish.1 = (bf16[256,1024]{1,0:T(8,128)(2,1)}, f32[256,1024]{1,0:T(8,128)}) custom-call(bf16[256,1024]{1,0:T(8,128)(2,1)} %get-tuple-element.4.codes, f32[256,1024]{1,0:T(8,128)} %get-tuple-element.5.total, s32[8,1024]{1,0:T(8,128)} %bitcast.3), custom_call_target="tpu_custom_call" | custom-call | flops 10000000 | bytes 3145728 | tf_op jit(solution)/shard_map/finish/pallas_call | solution.py:370

commit v4 on v3

--- a/solution.py
+++ b/solution.py
@@ -9,7 +9,7 @@
 NX, NY, NZ = 4, 4, 16
 FAR = (8, 7, 9, 6, 10, 5, 11, 4, 12, 3, 13, 2, 14, 1, 15, 0)
 OFFS = (2, 1, 3)
-SPLIT = 2
+LATE = 4
 BF, F32 = jnp.bfloat16, jnp.float32
 
 
@@ -110,24 +110,24 @@
                 out[g, xx * 16 + zz] = value[top : top + 16, left : left + 128]
 
     products(1 - c, 0, psend, BF)
+    pl.semaphore_wait(barrier, len(everyone))
+    send(psend.at[0], precv.at[0], s_p, r_p.at[0], partner)
     products(1 - c, 1, psend, BF)
-    pl.semaphore_wait(barrier, len(everyone))
-    send(psend, precv, s_p, r_p, partner)
+    send(psend.at[1], precv.at[1], s_p, r_p.at[1], partner)
     own_batch = batch.at[pl.ds(mine, 256), :]
     for k in range(3):
         send(own_batch, own_batch, s_b, r_b.at[k], ypeer[k])
-    products(c, 0, pown, F32)
-    products(c, 1, pown, F32)
-
-    arrived(precv, r_p)
-    for j in range(4):
-        for k in range(3):
-            for q in range(4):
-                t = xs[k] * 16 + zs[4 * j + q]
-                for g in range(2):
-                    xsend[k, 4 * j + q, g] = (pown[g, t] + precv[g, t].astype(F32)).astype(BF)
-            piece = pl.ds(4 * j, 4)
-            send(xsend.at[k, piece], xrecv.at[k, piece], s_x, r_x.at[j], xpeer[k])
+
+    for g in range(2):
+        products(c, g, pown, F32)
+        arrived(precv.at[g], r_p.at[g])
+        for j in range(2):
+            piece = pl.ds(8 * j, 8)
+            for k in range(3):
+                for n in range(8 * j, 8 * j + 8):
+                    t = xs[k] * 16 + zs[n]
+                    xsend[k, g, n] = (pown[g, t] + precv[g, t].astype(F32)).astype(BF)
+                send(xsend.at[k, g, piece], xrecv.at[k, g, piece], s_x, r_x.at[g, j], xpeer[k])
 
     for j in range(8):
         kept = masked[128 * j : 128 * (j + 1), :].astype(F32)
@@ -138,22 +138,20 @@
         e_own[j : j + 1, :] = jnp.sum(jnp.transpose(part), axis=0, keepdims=True)
     send(e_own, e_core, s_e.at[0], r_e.at[0], partner)
 
-    for j in range(4):
-        arrived(xrecv.at[:, 4 * j : 4 * j + 4], r_x.at[j])
-        for q in range(4):
-            n = 4 * j + q
-            t = x * 16 + zs[n]
-            for g in range(2):
+    for g in range(2):
+        for j in range(2):
+            arrived(xrecv.at[:, g, 8 * j : 8 * j + 8], r_x.at[g, j])
+            for n in range(8 * j, 8 * j + 8):
+                t = x * 16 + zs[n]
                 added = pown[g, t] + precv[g, t].astype(F32)
                 for k in range(3):
-                    added += xrecv[k, n, g].astype(F32)
+                    added += xrecv[k, g, n].astype(F32)
                 if n < 15:
-                    zsend[n, g] = added.astype(BF)
+                    zsend[g, n] = added.astype(BF)
+                    send(zsend.at[g, n], zrecv.at[g, n], s_z, r_z.at[g], zpeer[n])
                 else:
                     zown[g] = added
-            if n < 15:
-                send(zsend.at[n], zrecv.at[n], s_z, r_z, zpeer[n])
-        if j == 0:
+        if g == 0:
             arrived(e_core, r_e.at[0])
             e_x[...] = e_own[...] + e_core[...]
             for k in range(3):
@@ -162,14 +160,14 @@
     e_z[...] = e_x[...] + e_xr[0] + e_xr[1] + e_xr[2]
     for n in range(15):
         send(e_z, e_zr.at[n], s_e.at[2], r_e.at[2], zpeer[n])
-    arrived(zrecv, r_z)
-    added = zown[...]
-    for n in range(15):
-        added += zrecv[n].astype(F32)
-    zall[15] = added.astype(BF)
-    size = 16 // SPLIT
-    for n in range(15):
-        send(zall.at[15], zall.at[n], s_a, r_a.at[n // size], zpeer[n])
+    for g in range(2):
+        arrived(zrecv.at[g], r_z.at[g])
+        added = zown[g]
+        for n in range(15):
+            added += zrecv[g, n].astype(F32)
+        zall[g, 15] = added.astype(BF)
+        for n in range(15):
+            send(zall.at[g, 15], zall.at[g, n], s_a, r_a.at[g, int(n >= LATE)], zpeer[n])
 
     arrived(e_zr, r_e.at[2])
     energy = e_z[...]
@@ -179,19 +177,24 @@
     block = c * 4 + x
     steps[...] = column(e_step[pl.ds(block, 1), :])
 
-    for j in reversed(range(SPLIT)):
-        arrived(zall.at[size * j : min(size * (j + 1), 15)], r_a.at[j])
-        for n in reversed(range(size * j, size * (j + 1))):
+    for j in (1, 0):
+        low, high = (LATE, 16) if j else (0, LATE)
+        slots = range(low, high)
+        piece = pl.ds(low, high - low)
+        arrived(zall.at[0, low : high - j], r_a.at[0, j])
+        for n in slots:
             came = (z + NZ - FAR[n]) % NZ
             step = steps[pl.ds(pl.multiple_of(16 * (came // 2), 16), 16), :]
-            fall[block, n] = shrink(zall[n, 0].astype(F32) * step, 0.3 * step).astype(BF)
-            gmat[y, n] = zall[n, 1]
-        piece = pl.ds(size * j, size)
-        own_f, own_g = fall.at[block, piece], gmat.at[y, piece]
+            fall[block, n] = shrink(zall[0, n].astype(F32) * step, 0.3 * step).astype(BF)
+        ref = fall.at[block, piece]
         for to in xpeer + xother + [partner]:
-            send(own_f, own_f, s_f, r_f, to)
+            send(ref, ref, s_f, r_f, to)
+        arrived(zall.at[1, low : high - j], r_a.at[1, j])
+        for n in slots:
+            gmat[y, n] = zall[1, n]
+        ref = gmat.at[y, piece]
         for k in range(3):
-            send(own_g, own_g, s_g, r_g, ypeer[k])
+            send(ref, ref, s_g, r_g, ypeer[k])
     arrived(fall.at[0:7], r_f)
     arrived(gmat.at[0:3], r_g)
 
@@ -203,7 +206,7 @@
         sides = [jnp.concatenate([tiles(at(row, half)) for row in range(8)], axis=0) for half in range(2)]
         return jnp.concatenate(sides, axis=1)
 
-    push = -matrix(lambda n: zall[n, 0]).astype(F32)
+    push = -matrix(lambda n: zall[0, n]).astype(F32)
     for g in range(4):
         left = matrix(lambda n: gmat[g, n])
         right = jnp.concatenate([matrix(lambda n: fall[2 * g + b, n]) for b in range(2)], axis=0)
@@ -299,7 +302,7 @@
         (e_zr, s_e.at[2]),
         (xsend, s_x),
         (zsend, s_z),
-        (zall.at[0:15], s_a),
+        (zall.at[:, 0:15], s_a),
         (fall.at[0:7], s_f),
         (gmat.at[0:3], s_g),
         (call.at[0:5, 0:768, :], s_c),
@@ -321,7 +324,7 @@
 def body(pool, dictionary, support, pick):
     dma = pltpu.SemaphoreType.DMA
     sems = [dma(()), dma((4,)), dma((2,)), dma(()), dma((2,))]
-    for shape in ((), (3,), (), (), (3,), (3,), (), (4,), (), (), (), (SPLIT,), (), (), (), (), (), (), (2, 3), (4, 2), (4,)):
+    for shape in ((), (3,), (), (2,), (3,), (3,), (), (2, 2), (), (2,), (), (2, 2), (), (), (), (), (), (), (2, 3), (4, 2), (4,)):
         sems.append(dma(shape))
     hbm = pl.BlockSpec(memory_space=pl.ANY)
     supt = jnp.transpose(support)
@@ -343,12 +346,12 @@
             pltpu.VMEM((2, 64, 16, 128), BF),
             pltpu.VMEM((2, 64, 16, 128), F32),
             pltpu.VMEM((2, 64, 16, 128), BF),
-            pltpu.VMEM((3, 16, 2, 16, 128), BF),
-            pltpu.VMEM((3, 16, 2, 16, 128), BF),
-            pltpu.VMEM((15, 2, 16, 128), BF),
-            pltpu.VMEM((15, 2, 16, 128), BF),
+            pltpu.VMEM((3, 2, 16, 16, 128), BF),
+            pltpu.VMEM((3, 2, 16, 16, 128), BF),
+            pltpu.VMEM((2, 15, 16, 128), BF),
+            pltpu.VMEM((2, 15, 16, 128), BF),
             pltpu.VMEM((2, 16, 128), F32),
-            pltpu.VMEM((16, 2, 16, 128), BF),
+            pltpu.VMEM((2, 16, 16, 128), BF),
             pltpu.VMEM((8, 128), F32),
             pltpu.VMEM((8, 128), F32),
             pltpu.VMEM((8, 128), F32),

time: 69 us -> 64.6 us (0.936)
  Pallas kernels: 68.2 us -> 63.8 us
    pallas_call x1, Pallas kernels: 65.7 us -> 61.3 us  [body(): pl.pallas_call(gather, out_shape=(jax.ShapeDtypeStruct((256, 1024), BF),...]
where the time goes in v4:
time: 64.6 us; the launch traced here: 64.4 us
  Pallas kernels  63.8 us (99%)
    pallas_call x1, Pallas kernels, body(): pl.pallas_call(gather, out_shape=(jax.ShapeDtypeStruct((256, 1024), BF),...  61.3 us
    pallas_call x1, Pallas kernels, body(): pl.pallas_call(finish, grid=(2,), out_shape=(jax.ShapeDtypeStruct((256, 1...  2.53 us

profile of v4, /device:TPU:1, one launch (start us, length us, event | category | flops | bytes accessed | tf_op | source)
XLA Modules:
  0.0 64.4 jit_solution(3429508621785401162)
XLA Ops:
  0.6 61.3 %gather.1 = (bf16[256,1024]{1,0:T(8,128)(2,1)}, f32[256,1024]{1,0:T(8,128)}) custom-call(bf16[512,1024]{1,0:T(8,128)(2,1)} %pool_in.1, bf16[1024,1024]{1,0:T(8,128)(2,1)} %dico_in.1, s32[8,1024]{1,0:T(8,128)} %bitcast.2, s32[1,256]{1,0:T(1,128)} %bitcast.4), custom_call_target="tpu_custom_call" | custom-call | flops 3000000000 | bytes 6291456 | tf_op jit(solution)/shard_map/gather/pallas_call | solution.py:331
  61.9 2.5 %finish.1 = (bf16[256,1024]{1,0:T(8,128)(2,1)}, f32[256,1024]{1,0:T(8,128)}) custom-call(bf16[256,1024]{1,0:T(8,128)(2,1)} %get-tuple-element.4.codes, f32[256,1024]{1,0:T(8,128)} %get-tuple-element.5.total, s32[8,1024]{1,0:T(8,128)} %bitcast.3), custom_call_target="tpu_custom_call" | custom-call | flops 10000000 | bytes 3145728 | tf_op jit(solution)/shard_map/finish/pallas_call | solution.py:373

commit v5 on v4

--- a/solution.py
+++ b/solution.py
@@ -37,7 +37,7 @@
 def gather(
     pool_in, dico_in, supt_in, pick_in, codes_out, total_out,
     pool, dico, supt, pick, call, batch, masked, group_out, total, psend, pown, precv, xsend, xrecv, zsend, zrecv, zown, zall,
-    e_own, e_core, e_x, e_xr, e_z, e_zr, e_step, steps, fall, gmat,
+    e_own, e_core, e_x, e_xr, e_z, e_zr, steps, fall, gmat,
     l_pool, l_dico, l_small, l_codes, l_total,
     s_b, r_b, s_p, r_p, s_e, r_e, s_x, r_x, s_z, r_z, s_a, r_a, s_f, r_f, s_g, r_g, s_c, s_cc, r_a0, r_all, r_cc,
 ):
@@ -135,8 +135,8 @@
         for b in range(8):
             piece = kept[:, 128 * b : 128 * (b + 1)]
             part += piece * piece
-        e_own[j : j + 1, :] = jnp.sum(jnp.transpose(part), axis=0, keepdims=True)
-    send(e_own, e_core, s_e.at[0], r_e.at[0], partner)
+        e_own[j] = jnp.sum(jnp.transpose(part), axis=0, keepdims=True)
+    send(e_own.at[pl.ds((1 - c) * 4, 4)], e_core, s_e.at[0], r_e.at[0], partner)
 
     for g in range(2):
         for j in range(2):
@@ -153,11 +153,11 @@
                     zown[g] = added
         if g == 0:
             arrived(e_core, r_e.at[0])
-            e_x[...] = e_own[...] + e_core[...]
+            e_x[...] = e_own[pl.ds(c * 4, 4)] + e_core[...]
             for k in range(3):
-                send(e_x, e_xr.at[k], s_e.at[1], r_e.at[1], xpeer[k])
+                send(e_x.at[xs[k]], e_xr.at[k], s_e.at[1], r_e.at[1], xpeer[k])
     arrived(e_xr, r_e.at[1])
-    e_z[...] = e_x[...] + e_xr[0] + e_xr[1] + e_xr[2]
+    e_z[...] = e_x[x] + e_xr[0] + e_xr[1] + e_xr[2]
     for n in range(15):
         send(e_z, e_zr.at[n], s_e.at[2], r_e.at[2], zpeer[n])
     for g in range(2):
@@ -173,9 +173,8 @@
     energy = e_z[...]
     for n in range(15):
         energy += e_zr[n]
-    e_step[...] = 1.0 / (energy + 1e-05)
     block = c * 4 + x
-    steps[...] = column(e_step[pl.ds(block, 1), :])
+    steps[...] = column(1.0 / (energy + 1e-05))
 
     for j in (1, 0):
         low, high = (LATE, 16) if j else (0, LATE)
@@ -297,7 +296,7 @@
     for ref, sem in (
         (batch.at[0:768, :], s_b),
         (psend, s_p),
-        (e_own, s_e.at[0]),
+        (e_core, s_e.at[0]),
         (e_xr, s_e.at[1]),
         (e_zr, s_e.at[2]),
         (xsend, s_x),
@@ -352,13 +351,12 @@
             pltpu.VMEM((2, 15, 16, 128), BF),
             pltpu.VMEM((2, 16, 128), F32),
             pltpu.VMEM((2, 16, 16, 128), BF),
-            pltpu.VMEM((8, 128), F32),
-            pltpu.VMEM((8, 128), F32),
-            pltpu.VMEM((8, 128), F32),
-            pltpu.VMEM((3, 8, 128), F32),
-            pltpu.VMEM((8, 128), F32),
-            pltpu.VMEM((15, 8, 128), F32),
-            pltpu.VMEM((8, 128), F32),
+            pltpu.VMEM((8, 1, 128), F32),
+            pltpu.VMEM((4, 1, 128), F32),
+            pltpu.VMEM((4, 1, 128), F32),
+            pltpu.VMEM((3, 1, 128), F32),
+            pltpu.VMEM((1, 128), F32),
+            pltpu.VMEM((15, 1, 128), F32),
             pltpu.VMEM((128, 128), F32),
             pltpu.VMEM((8, 16, 16, 128), BF),
             pltpu.VMEM((4, 16, 16, 128), BF),

time: 64.6 us -> 64.6 us (level)
  no operation moved by 1% of the time
where the time goes in v5:
time: 64.6 us; the launch traced here: 64.4 us
  Pallas kernels  63.8 us (99%)
    pallas_call x1, Pallas kernels, body(): pl.pallas_call(gather, out_shape=(jax.ShapeDtypeStruct((256, 1024), BF),...  61.3 us
    pallas_call x1, Pallas kernels, body(): pl.pallas_call(finish, grid=(2,), out_shape=(jax.ShapeDtypeStruct((256, 1...  2.52 us

profile of v5, /device:TPU:1, one launch (start us, length us, event | category | flops | bytes accessed | tf_op | source)
XLA Modules:
  0.0 64.4 jit_solution(4174238498889136218)
XLA Ops:
  0.6 61.3 %gather.1 = (bf16[256,1024]{1,0:T(8,128)(2,1)}, f32[256,1024]{1,0:T(8,128)}) custom-call(bf16[512,1024]{1,0:T(8,128)(2,1)} %pool_in.1, bf16[1024,1024]{1,0:T(8,128)(2,1)} %dico_in.1, s32[8,1024]{1,0:T(8,128)} %bitcast.2, s32[1,256]{1,0:T(1,128)} %bitcast.4), custom_call_target="tpu_custom_call" | custom-call | flops 3000000000 | bytes 6291456 | tf_op jit(solution)/shard_map/gather/pallas_call | solution.py:330
  61.9 2.5 %finish.1 = (bf16[256,1024]{1,0:T(8,128)(2,1)}, f32[256,1024]{1,0:T(8,128)}) custom-call(bf16[256,1024]{1,0:T(8,128)(2,1)} %get-tuple-element.4.codes, f32[256,1024]{1,0:T(8,128)} %get-tuple-element.5.total, s32[8,1024]{1,0:T(8,128)} %bitcast.3), custom_call_target="tpu_custom_call" | custom-call | flops 10000000 | bytes 3145728 | tf_op jit(solution)/shard_map/finish/pallas_call | solution.py:371

commit v6 on v5

--- a/solution.py
+++ b/solution.py
@@ -39,7 +39,7 @@
     pool, dico, supt, pick, call, batch, masked, group_out, total, psend, pown, precv, xsend, xrecv, zsend, zrecv, zown, zall,
     e_own, e_core, e_x, e_xr, e_z, e_zr, steps, fall, gmat,
     l_pool, l_dico, l_small, l_codes, l_total,
-    s_b, r_b, s_p, r_p, s_e, r_e, s_x, r_x, s_z, r_z, s_a, r_a, s_f, r_f, s_g, r_g, s_c, s_cc, r_a0, r_all, r_cc,
+    s_b, r_b, s_p, r_p, s_e, r_e, s_x, r_x, s_z, r_z, s_a, r_a, s_f, r_f, s_fc, r_fc, s_g, r_g, s_c, s_cc, r_a0, r_all, r_cc,
 ):
     y, v = lax.axis_index("frame"), lax.axis_index("vox")
     x, z, c = v // 32, (v // 2) % NZ, v % 2
@@ -51,7 +51,6 @@
     xs = [(x + i) % NX for i in OFFS]
     zs = [(z + o) % NZ for o in FAR]
     xpeer = [dev(xx, y, z, c) for xx in xs]
-    xother = [dev(xx, y, z, 1 - c) for xx in xs]
     ypeer = [dev(x, (y + i) % NY, z, c) for i in OFFS]
     zpeer = [dev(x, y, zz, c) for zz in zs[:15]]
 
@@ -76,7 +75,7 @@
         load_dico.append(pltpu.make_async_copy(dico_in.at[rows], dico.at[rows], l_dico.at[j]))
         load_dico[j].start()
     barrier = pltpu.get_barrier_semaphore()
-    everyone = [partner] + xpeer + xother + ypeer + zpeer
+    everyone = zpeer + xpeer + ypeer + [partner]
     for to in everyone:
         pl.semaphore_signal(barrier, inc=1, device_id=to, device_id_type=MESH)
 
@@ -109,11 +108,11 @@
                 left = 128 * (zz % 2)
                 out[g, xx * 16 + zz] = value[top : top + 16, left : left + 128]
 
-    products(1 - c, 0, psend, BF)
+    for g in range(2):
+        products(1 - c, g, psend, BF)
     pl.semaphore_wait(barrier, len(everyone))
-    send(psend.at[0], precv.at[0], s_p, r_p.at[0], partner)
-    products(1 - c, 1, psend, BF)
-    send(psend.at[1], precv.at[1], s_p, r_p.at[1], partner)
+    for g in range(2):
+        send(psend.at[g], precv.at[g], s_p, r_p.at[g], partner)
     own_batch = batch.at[pl.ds(mine, 256), :]
     for k in range(3):
         send(own_batch, own_batch, s_b, r_b.at[k], ypeer[k])
@@ -176,25 +175,38 @@
     block = c * 4 + x
     steps[...] = column(1.0 / (energy + 1e-05))
 
+    def swap(j):
+        low, high = (LATE, 16) if j else (0, LATE)
+        piece = pl.ds(low, high - low)
+        arrived(fall.at[0:3, piece], r_f.at[j])
+        ref = fall.at[pl.ds(c * 4, 4), piece]
+        send(ref, ref, s_fc, r_fc.at[j], partner)
+
     for j in (1, 0):
         low, high = (LATE, 16) if j else (0, LATE)
         slots = range(low, high)
         piece = pl.ds(low, high - low)
-        arrived(zall.at[0, low : high - j], r_a.at[0, j])
-        for n in slots:
-            came = (z + NZ - FAR[n]) % NZ
-            step = steps[pl.ds(pl.multiple_of(16 * (came // 2), 16), 16), :]
-            fall[block, n] = shrink(zall[0, n].astype(F32) * step, 0.3 * step).astype(BF)
-        ref = fall.at[block, piece]
-        for to in xpeer + xother + [partner]:
-            send(ref, ref, s_f, r_f, to)
-        arrived(zall.at[1, low : high - j], r_a.at[1, j])
-        for n in slots:
-            gmat[y, n] = zall[1, n]
-        ref = gmat.at[y, piece]
-        for k in range(3):
-            send(ref, ref, s_g, r_g, ypeer[k])
-    arrived(fall.at[0:7], r_f)
+        for g in range(2):
+            arrived(zall.at[g, low : high - j], r_a.at[g, j])
+            if g == 0:
+                for n in slots:
+                    came = (z + NZ - FAR[n]) % NZ
+                    step = steps[pl.ds(pl.multiple_of(16 * (came // 2), 16), 16), :]
+                    fall[block, n] = shrink(zall[0, n].astype(F32) * step, 0.3 * step).astype(BF)
+                ref = fall.at[block, piece]
+                for to in xpeer:
+                    send(ref, ref, s_f, r_f.at[j], to)
+                if j == 0:
+                    swap(1)
+            else:
+                for n in slots:
+                    gmat[y, n] = zall[1, n]
+                ref = gmat.at[y, piece]
+                for k in range(3):
+                    send(ref, ref, s_g, r_g, ypeer[k])
+    swap(0)
+    arrived(fall.at[0:4, LATE:16], r_fc.at[1])
+    arrived(fall.at[0:4, 0:LATE], r_fc.at[0])
     arrived(gmat.at[0:3], r_g)
 
     def at(row, half):
@@ -302,7 +314,8 @@
         (xsend, s_x),
         (zsend, s_z),
         (zall.at[:, 0:15], s_a),
-        (fall.at[0:7], s_f),
+        (fall.at[0:3], s_f),
+        (fall.at[0:4], s_fc),
         (gmat.at[0:3], s_g),
         (call.at[0:5, 0:768, :], s_c),
         (call.at[0:4], s_cc),
@@ -323,7 +336,7 @@
 def body(pool, dictionary, support, pick):
     dma = pltpu.SemaphoreType.DMA
     sems = [dma(()), dma((4,)), dma((2,)), dma(()), dma((2,))]
-    for shape in ((), (3,), (), (2,), (3,), (3,), (), (2, 2), (), (2,), (), (2, 2), (), (), (), (), (), (), (2, 3), (4, 2), (4,)):
+    for shape in ((), (3,), (), (2,), (3,), (3,), (), (2, 2), (), (2,), (), (2, 2), (), (2,), (), (2,), (), (), (), (), (2, 3), (4, 2), (4,)):
         sems.append(dma(shape))
     hbm = pl.BlockSpec(memory_space=pl.ANY)
     supt = jnp.transpose(support)

time: 64.6 us -> 63.8 us (0.988)
  Pallas kernels: 63.8 us -> 63 us
    pallas_call x1, Pallas kernels: 61.3 us -> 60.5 us  [body(): pl.pallas_call(gather, out_shape=(jax.ShapeDtypeStruct((256, 1024), BF),...]
where the time goes in v6:
time: 63.8 us; the launch traced here: 63.6 us
  Pallas kernels  63 us (99%)
  between operations  0.64 us (1%)
    pallas_call x1, Pallas kernels, body(): pl.pallas_call(gather, out_shape=(jax.ShapeDtypeStruct((256, 1024), BF),...  60.5 us
    pallas_call x1, Pallas kernels, body(): pl.pallas_call(finish, grid=(2,), out_shape=(jax.ShapeDtypeStruct((256, 1...  2.52 us

profile of v6, /device:TPU:1, one launch (start us, length us, event | category | flops | bytes accessed | tf_op | source)
XLA Modules:
  0.0 63.6 jit_solution(8661426643292829672)
XLA Ops:
  0.6 60.5 %gather.1 = (bf16[256,1024]{1,0:T(8,128)(2,1)}, f32[256,1024]{1,0:T(8,128)}) custom-call(bf16[512,1024]{1,0:T(8,128)(2,1)} %pool_in.1, bf16[1024,1024]{1,0:T(8,128)(2,1)} %dico_in.1, s32[8,1024]{1,0:T(8,128)} %bitcast.2, s32[1,256]{1,0:T(1,128)} %bitcast.4), custom_call_target="tpu_custom_call" | custom-call | flops 3000000000 | bytes 6291456 | tf_op jit(solution)/shard_map/gather/pallas_call | solution.py:343
  61.1 2.5 %finish.1 = (bf16[256,1024]{1,0:T(8,128)(2,1)}, f32[256,1024]{1,0:T(8,128)}) custom-call(bf16[256,1024]{1,0:T(8,128)(2,1)} %get-tuple-element.4.codes, f32[256,1024]{1,0:T(8,128)} %get-tuple-element.5.total, s32[8,1024]{1,0:T(8,128)} %bitcast.3), custom_call_target="tpu_custom_call" | custom-call | flops 10000000 | bytes 3145728 | tf_op jit(solution)/shard_map/finish/pallas_call | solution.py:384
